TPU v7x, 32 devices: a whole 2x2x4 slice. The times are simulated.
32 devices in a mesh: groups: 2 (over y), ep: 8 (over z, core), fsdp: 2 (over x).
Axes of the slice: x: 2, y: 2, z: 4, core: 2. Of those that a mesh axis runs over, the one named last changes fastest.
Arguments:
- tokens: bfloat16 [1024, 3072], P(('groups', 'ep'), 'fsdp'), parts along dimension 0, may hold values from -6 to 6
- cotangent: bfloat16 [1024, 3072], P(('groups', 'ep'), 'fsdp'), parts along dimension 0, may hold values from -6 to 6
- routes: int32 [1024, 4], P(('groups', 'ep')), parts along dimension 0, may hold values from 0 to 7, all different within a row; in each aligned block of 64 rows (0 to 63, 64 to 127, ...) at most 64 rows name the same one
- route_scale: int32 [1024, 4], P(('groups', 'ep')), parts along dimension 0, may hold values from 256 to 4096
- gate_weight: bfloat16 [8, 3072, 5376], P('ep', None, 'fsdp'), may hold values from -0.109375 to 0.109375
- up_weight: bfloat16 [8, 3072, 5376], P('ep', None, 'fsdp'), may hold values from -0.109375 to 0.109375
- down_weight: bfloat16 [8, 5376, 3072], P('ep', 'fsdp'), may hold values from -0.078125 to 0.078125
Outputs:
- token_grad: bfloat16 [1024, 3072], P(('groups', 'ep'), 'fsdp'), parts along dimension 0
- route_grad: float32 [1024, 4], P(('groups', 'ep')), parts along dimension 0
There are 2 independent parts, one for each index of `groups`. A program takes and returns all parts, laid end to end along the dimension named above; an argument that names none is the same for every part. Nothing has to cross between parts.
Inputs may be any that keep to these rules, and one draw needn't show every extreme that they name: `routes`: each row names 4 different experts; among the 64 rows of one index of ep no expert is named by more than 64 rows, and in every draw some expert is named by exactly 64 rows of some index.
All inputs are finite; a program needn't handle non-finite values.
Results may differ from a plain program's by a relative error of at most 0.0049.
Values may be sent and summed in bfloat16 or wider, within the bound.
A program may use at most 192 MiB of HBM per device.

v0:
```python
import math

import jax
import jax.numpy as jnp
from jax import lax
from jax.sharding import PartitionSpec as P

FF = 5376


def contract_last(left, right):
    return lax.dot_general(
        left, right, (((1,), (1,)), ((), ())), preferred_element_type=jnp.float32
    )


def shards(tokens, cotangent, routes, route_scale, gate_weight, up_weight, down_weight):
    ep_count = lax.axis_size("ep")
    expert_index = lax.axis_index("ep")
    row_count = tokens.shape[0]
    top_count = routes.shape[1]
    slot_cap = min(row_count, 2 * row_count * top_count // ep_count)
    capacity = ep_count * slot_cap
    full_tok, full_cot = (
        lax.all_gather(tokens, "fsdp", axis=1, tiled=True),
        lax.all_gather(cotangent, "fsdp", axis=1, tiled=True),
    )
    all_tok, all_cot = (
        lax.all_gather(full_tok, "ep", axis=0, tiled=True),
        lax.all_gather(full_cot, "ep", axis=0, tiled=True),
    )
    all_routes, all_scale = (
        lax.all_gather(routes, "ep", axis=0, tiled=True),
        lax.all_gather(route_scale, "ep", axis=0, tiled=True),
    )
    matched = all_routes == expert_index
    chosen = jnp.any(matched, axis=1)
    picked = chosen.astype(jnp.int32).reshape(ep_count, row_count)
    ranking = (jnp.cumsum(picked, axis=1) - picked).reshape(-1)
    blocks = jnp.arange(ep_count * row_count, dtype=jnp.int32) // row_count
    slot_index = jnp.where(chosen, blocks * slot_cap + ranking, capacity)
    positions = jnp.arange(ep_count * row_count, dtype=jnp.int32)
    source = jnp.zeros((capacity,), jnp.int32).at[slot_index].set(positions, mode="drop")
    token_weight = jnp.sum(jnp.where(matched, all_scale.astype(jnp.float32) / 4096.0, 0.0), axis=1)
    slot_weight = jnp.zeros((capacity,), jnp.float32).at[slot_index].set(token_weight, mode="drop")
    tile_tok = all_tok[source]
    tile_cot = all_cot[source]
    gate_here = gate_weight[0]
    up_here = up_weight[0]
    down_here = down_weight[0]
    gate_proj = jnp.dot(tile_tok, gate_here, preferred_element_type=jnp.float32)
    upward = jnp.dot(tile_tok, up_here, preferred_element_type=jnp.float32)
    backward = contract_last(tile_cot, down_here)
    sigmoid_gate = jax.nn.sigmoid(gate_proj)
    activated = gate_proj * sigmoid_gate
    route_part = jnp.sum(activated * upward * backward, axis=1) * (1.0 / math.sqrt(FF))
    scaled = slot_weight[:, None] * backward
    up_grad = (scaled * activated).astype(jnp.bfloat16)
    gate_grad = (scaled * upward * sigmoid_gate * (1.0 + gate_proj * (1.0 - sigmoid_gate))).astype(
        jnp.bfloat16
    )
    partial_value = contract_last(gate_grad, gate_here) + contract_last(up_grad, up_here)
    reduced = lax.psum_scatter(partial_value, "fsdp", scatter_dimension=1, tiled=True)
    route_tile = lax.psum(route_part, "fsdp")
    clipped = jnp.minimum(slot_index, capacity - 1)
    contrib = jnp.where(chosen[:, None], reduced[clipped], 0.0)
    route_contrib = jnp.where(matched, route_tile[clipped][:, None], 0.0)
    token_sum, route_sum = (
        lax.psum_scatter(contrib, "ep", scatter_dimension=0, tiled=True),
        lax.psum_scatter(route_contrib, "ep", scatter_dimension=0, tiled=True),
    )
    return (token_sum.astype(jnp.bfloat16), route_sum)


def solution(mesh):
    in_specs = (
        P(("groups", "ep"), "fsdp"),
        P(("groups", "ep"), "fsdp"),
        P(("groups", "ep"), None),
        P(("groups", "ep"), None),
        P("ep", None, "fsdp"),
        P("ep", None, "fsdp"),
        P("ep", "fsdp", None),
    )
    out_specs = (P(("groups", "ep"), "fsdp"), P(("groups", "ep"), None))
    return jax.shard_map(shards, mesh=mesh, in_specs=in_specs, out_specs=out_specs, check_vma=False)
```

profile of v0, /device:TPU:0, one launch (start us, length us, event | category | flops | bytes accessed | tf_op | source)
XLA Modules:
  0.0 341.8 jit_solution(2506626227176861366)
XLA Ops:
  7.2 0.0 all-gather.7.cloned.1.call-start
  7.2 10.4 %all_gather.22 = bf16[64,3072]{1,0:T(8,128)(2,1)} all-gather(bf16[64,1536]{1,0:T(8,128)(2,1)} %param.7), channel_id=1, replica_groups=mesh['groups'=2,'ep'=8,'fsdp'=2] {'fsdp'}, dimensions={1}, use_global_device_ids=true | all-gather | bytes 589824 | tf_op jit(solution)/shard_map/all_gather | solution.py:25
  17.6 0.0 all-gather.7.cloned.1.call-update
  17.6 0.0 all-gather.5.cloned.1.call-start
  17.7 7.1 %all_gather.20 = bf16[64,3072]{1,0:T(8,128)(2,1)} all-gather(bf16[64,1536]{1,0:T(8,128)(2,1)} %param.8), channel_id=1, replica_groups=mesh['groups'=2,'ep'=8,'fsdp'=2] {'fsdp'}, dimensions={1}, use_global_device_ids=true | all-gather | bytes 589824 | tf_op jit(solution)/shard_map/all_gather | solution.py:26
  24.8 0.0 all-gather.5.cloned.1.call-update
  24.8 0.0 reduce-scatter.6.cloned.1.call-start
  24.9 13.7 %all-gather = s32[8,64,4]{1,2,0:T(4,128)S(1)} all-gather(s32[1,64,4]{1,2,0:T(4,128)} %bitcast.32), channel_id=1, replica_groups=mesh['groups'=2,'ep'=8,'fsdp'=2] {'ep'}, dimensions={0}, use_global_device_ids=true | all-gather | bytes 9216 | tf_op jit(solution)/shard_map/all_gather | solution.py:33
  38.6 0.1 reshape.161
  38.7 0.1 reduce_or.12
  38.8 0.1 reshape.159
  38.9 0.1 reshape.103
  39.0 0.2 reduce_window_sum.13
  39.2 0.1 reduce_window_sum.14
  39.3 2.4 scatter_custom_fusion.1
  41.8 13.0 %all-gather.1 = s32[8,64,4]{1,2,0:T(4,128)S(1)} all-gather(s32[1,64,4]{1,2,0:T(4,128)} %bitcast.33), channel_id=1, replica_groups=mesh['groups'=2,'ep'=8,'fsdp'=2] {'ep'}, dimensions={0}, use_global_device_ids=true | all-gather | bytes 9216 | tf_op jit(solution)/shard_map/all_gather | solution.py:34
  54.8 0.1 reshape.163
  54.9 1.8 all-gather.7.cloned.1.call-done
  56.7 8.4 %gather_fusion.1 = bf16[512,3072]{1,0:T(8,128)(2,1)S(1)} fusion(bf16[512,3072]{1,0:T(8,128)(2,1)} %all-gather.7.cloned.1.call-done, s32[1024]{0:T(1024)S(1)} %pad_clamp_fusion.1), kind=kCustom, calls=%fused_computation.1 | custom fusion | bytes 6293504 | tf_op jit(solution)/shard_map/gather | solution.py:46
  65.1 15.2 %fusion.2 = f32[512,2688]{1,0:T(8,128)} fusion(bf16[512,3072]{1,0:T(8,128)(2,1)S(1)} %gather_fusion.1, bf16[1,3072,2688]{2,1,0:T(8,128)(2,1)} %param.11), kind=kOutput, calls=%fused_computation.8 | convolution fusion | flops 8455716864 | bytes 25165824 | tf_op jit(solution)/shard_map/dot_general | solution.py:51
  80.3 15.2 %fusion.6 = f32[512,2688]{1,0:T(8,128)} fusion(bf16[512,3072]{1,0:T(8,128)(2,1)S(1)} %gather_fusion.1, bf16[1,3072,2688]{2,1,0:T(8,128)(2,1)} %param.12), kind=kOutput, calls=%fused_computation.12 | convolution fusion | flops 8455716864 | bytes 25165824 | tf_op jit(solution)/shard_map/dot_general | solution.py:52
  95.4 0.1 all-gather.5.cloned.1.call-done
  95.5 8.6 %gather_fusion = bf16[512,3072]{1,0:T(8,128)(2,1)S(1)} fusion(bf16[512,3072]{1,0:T(8,128)(2,1)} %all-gather.5.cloned.1.call-done, s32[1024]{0:T(1024)S(1)} %pad_clamp_fusion.1), kind=kCustom, calls=%fused_computation | custom fusion | bytes 6293504 | tf_op jit(solution)/shard_map/gather | solution.py:47
  104.1 29.7 %multiply_reduce_fusion = (f32[512]{0:T(512)S(1)}, f32[512,2688]{1,0:T(8,128)}) fusion(f32[512,2688]{1,0:T(8,128)} %fusion.6, f32[512,2688]{1,0:T(8,128)} %fusion.2, bf16[512,3072]{1,0:T(8,128)(2,1)S(1)} %gather_fusion, bf16[1,2688,3072]{2,1,0:T(8,128)(2,1)} %param.13), kind=kOutput, calls=%fused_computation.16 | convolution fusion | flops 8465350144 | bytes 36177920 | tf_op jit(solution)/shard_map/dot_general | solution.py:12
  133.8 4.9 %psum.7 = f32[512]{0:T(512)S(1)} all-reduce(f32[512]{0:T(512)S(1)} %broadcast_multiply_fusion), channel_id=1, replica_groups=mesh['groups'=2,'ep'=8,'fsdp'=2] {'fsdp'}, use_global_device_ids=true, to_apply=%region_8.9 | all-reduce | flops 512 | bytes 4096 | tf_op jit(solution)/shard_map/psum | solution.py:64
  138.7 3.5 %gather_fusion.3 = f32[512]{0:T(512)S(1)} fusion(f32[512]{0:T(512)S(1)} %psum.7, s32[1024]{0:T(1024)S(1)} %pad_clamp_fusion), kind=kCustom, calls=%fused_computation.3 | custom fusion | bytes 6144 | tf_op jit(solution)/shard_map/gather | solution.py:67
  142.3 2.4 scatter_custom_fusion
  144.7 20.7 %fusion = f32[512,3072]{1,0:T(8,128)} fusion(bf16[1,3072,2688]{2,1,0:T(8,128)(2,1)} %param.11, f32[512,2688]{1,0:T(8,128)} %fusion.2, f32[512,2688]{1,0:T(8,128)} %fusion.6, f32[512,2688]{1,0:T(8,128)} %get-tuple-element.9, f32[512]{0:T(512)S(1)} %scatter_custom_fusion), kind=kOutput, calls=%fused_computation.6 | convolution fusion | flops 8470855680 | bytes 39323648 | tf_op jit(solution)/shard_map/dot_general | solution.py:12
  165.4 18.5 %fusion.11 = f32[512,3072]{1,0:T(8,128)} fusion(f32[512,3072]{1,0:T(8,128)} %fusion, bf16[1,3072,2688]{2,1,0:T(8,128)(2,1)} %param.12, f32[512,2688]{1,0:T(8,128)} %get-tuple-element.9, f32[512]{0:T(512)S(1)} %scatter_custom_fusion, f32[512,2688]{1,0:T(8,128)} %fusion.2), kind=kOutput, calls=%fused_computation.21 | convolution fusion | flops 8466923520 | bytes 40110080 | tf_op jit(solution)/shard_map/dot_general | solution.py:12
  183.9 0.0 reduce-scatter.6.cloned.1.call-update
  183.9 0.0 reduce-scatter.10.cloned.1.call-start
  183.9 0.9 copy.17
  184.8 0.0 reduce-scatter.10.cloned.1.call-update
  184.8 0.0 reduce-scatter.8.cloned.1.call-start
  184.9 75.4 %reduce-scatter.6.cloned.1.call-done = f32[512,1536]{1,0:T(8,128)} async-done(((f32[512,3072]{1,0:T(8,128)}), f32[512,1536]{1,0:T(8,128)}) %reduce-scatter.6.cloned.1.call-update) | async-done | bytes 3145744 | tf_op jit(solution)/shard_map/reduce_scatter | solution.py:63
  260.3 5.6 %gather_fusion.2 = f32[512,1536]{1,0:T(8,128)S(1)} fusion(f32[512,1536]{1,0:T(8,128)} %reduce-scatter.6.cloned.1.call-done, s32[1024]{0:T(1024)S(1)} %pad_clamp_fusion), kind=kCustom, calls=%fused_computation.2 | custom fusion | bytes 6293504 | tf_op jit(solution)/shard_map/gather | solution.py:66
  265.9 1.9 broadcast_select_fusion
  267.8 0.0 reduce-scatter.8.cloned.1.call-update
  267.9 25.1 %reduce-scatter.10.cloned.1.call-done = f32[64,4]{1,0:T(8,128)} async-done(((f32[512,4]{1,0:T(8,128)}), f32[64,4]{1,0:T(8,128)}) %reduce-scatter.10.cloned.1.call-update) | async-done | bytes 1040
  293.0 1.4 copy.18
  294.4 39.2 %reduce-scatter.8.cloned.1.call-done = f32[64,1536]{1,0:T(8,128)} async-done(((f32[512,1536]{1,0:T(8,128)}), f32[64,1536]{1,0:T(8,128)}) %reduce-scatter.8.cloned.1.call-update) | async-done | bytes 393232 | tf_op jit(solution)/shard_map/reduce_scatter | solution.py:69
  333.6 1.7 convert_element_type.39
  (12 shorter events, 0.1 us)
Async XLA Ops:
  7.2 49.5 %all-gather.7.cloned.1.call-start = ((), (), s32[]{:S(2)}) async-start(), calls=%async_computation.4 | async-start | bytes 3538944 | tf_op jit(solution)/shard_map/all_gather | solution.py:29
  17.6 77.8 %all-gather.5.cloned.1.call-start = ((), (), s32[]{:S(2)}) async-start(), calls=%async_computation.3 | async-start | bytes 3538944 | tf_op jit(solution)/shard_map/all_gather | solution.py:30
  24.8 235.5 %reduce-scatter.6.cloned.1.call-start = ((), (), s32[]{:S(2)}) async-start(), calls=%async_computation.5 | async-start | bytes 9437184 | tf_op jit(solution)/shard_map/reduce_scatter | solution.py:63
  183.9 109.1 %reduce-scatter.10.cloned.1.call-start = ((), (), s32[]{:S(2)}) async-start(), calls=%async_computation.7 | async-start | bytes 294912
  184.8 148.7 %reduce-scatter.8.cloned.1.call-start = ((), (), s32[]{:S(2)}) async-start(), calls=%async_computation.6 | async-start | bytes 3538944 | tf_op jit(solution)/shard_map/reduce_scatter | solution.py:69
Sparse Core Ops, SparseCore 0:
  17.8 38.8 all-gather.6
  58.3 37.1 all-gather.4
  184.0 76.2 reduce-scatter.5
  262.5 30.4 reduce-scatter.9
  295.1 38.4 reduce-scatter.7
where the time goes:
time: 342 us
  waiting for transfers between devices  142 us (42%)
  matrix products  99.3 us (29%)
  blocking collectives  49.2 us (14%)
  local copies, waits for them, and re-layouts  33.7 us (10%)
  between operations  13.9 us (4%)
  other arithmetic  3.96 us (1%)
    reduce_scatter x1, waiting for transfers between devices, shards(): lax.psum_scatter(partial_value, 'fsdp', scatter_dimension=1, tiled=True)  75.4 us
    dot_general x3, matrix products, contract_last(): lax.dot_general(left, right, (((1,), (1,)), ((), ())), preferred_element_...  68.9 us
    reduce_scatter x1, waiting for transfers between devices, shards(): lax.psum_scatter(contrib, 'ep', scatter_dimension=0, tiled=True)  39.2 us
    unnamed x6, waiting for transfers between devices  25.2 us
    dot_general x1, matrix products, shards(): upward = jnp.dot(tile_tok, up_here, preferred_element_type=jnp.float32)  15.2 us
    dot_general x1, matrix products, shards(): gate_proj = jnp.dot(tile_tok, gate_here, preferred_element_type=jnp.float32)  15.2 us
    all_gather x1, blocking collectives, shards(): lax.all_gather(routes, 'ep', axis=0, tiled=True)  13.7 us
    all_gather x1, blocking collectives, shards(): lax.all_gather(route_scale, 'ep', axis=0, tiled=True)  13 us
  transfers between devices with their start and end apart: 5, of which 5 were waited for; matrix products, arithmetic and copies ran while one was open for 15% of the time, Pallas kernels for 0%

commit v1 on v0

v1 whole, which is shorter than its diff:
```python
import functools
import math

import jax
import jax.numpy as jnp
from jax import lax
from jax.experimental import pallas as pl
from jax.experimental.pallas import tpu as pltpu
from jax.sharding import PartitionSpec as P

FF = 5376
MESH = pl.DeviceIdType.MESH
LANES = 128
TILE = 512


def contract_last(left, right):
    return lax.dot_general(
        left, right, (((1,), (1,)), ((), ())), preferred_element_type=jnp.float32
    )


def kernel(
    nz, nx, widths, tok_ref, cot_ref, routes_ref, scale_ref, wg_hbm, wu_hbm, wd_hbm,
    out_ref, rg_ref,
    X, Wg, Wu, Wd, acc, rp, wv, WS, WR, RS, RR, SC, RC, SX, RX, S2, SZ, RZ,
    wsem, zs, zr, xs, xr, cs, cr, bs, br, ps, pr, ccs, ccr, cxs, cxr, czs, czr,
):
    ep = 2 * nz
    n = ep * nx
    nt = len(widths)
    dx = tok_ref.shape[1]
    hr = tok_ref.shape[0] // 2
    mine = nz * hr
    g = lax.axis_index("groups")
    e = lax.axis_index("ep")
    x = lax.axis_index("fsdp")
    z, c = lax.div(e, 2), lax.rem(e, 2)
    me = e * nx + x

    def rows(cc, zz, count=1):
        return pl.ds(pl.multiple_of((cc * nz + zz) * hr, hr), hr * count)

    def cols(xx):
        return pl.ds(pl.multiple_of(xx * dx, LANES), dx)

    def remote(src, dst, ss, rs, dev):
        return pltpu.make_async_remote_copy(
            src_ref=src, dst_ref=dst, send_sem=ss, recv_sem=rs,
            device_id=dev, device_id_type=MESH,
        )

    def tile_copies(t, slot):
        w, off = widths[t], sum(widths[:t])
        return (
            pltpu.make_async_copy(wg_hbm.at[0, :, pl.ds(off, w)], Wg.at[slot, :, pl.ds(0, w)], wsem.at[slot, 0]),
            pltpu.make_async_copy(wu_hbm.at[0, :, pl.ds(off, w)], Wu.at[slot, :, pl.ds(0, w)], wsem.at[slot, 1]),
            pltpu.make_async_copy(wd_hbm.at[0, pl.ds(off, w), :], Wd.at[slot, pl.ds(0, w), :], wsem.at[slot, 2]),
        )

    def main_copies(t, slot):
        w = widths[0]
        off = pl.multiple_of(t * w, w)
        return (
            pltpu.make_async_copy(wg_hbm.at[0, :, pl.ds(off, w)], Wg.at[slot, :, pl.ds(0, w)], wsem.at[slot, 0]),
            pltpu.make_async_copy(wu_hbm.at[0, :, pl.ds(off, w)], Wu.at[slot, :, pl.ds(0, w)], wsem.at[slot, 1]),
            pltpu.make_async_copy(wd_hbm.at[0, pl.ds(off, w), :], Wd.at[slot, pl.ds(0, w), :], wsem.at[slot, 2]),
        )

    for copy in tile_copies(0, 0):
        copy.start()

    for h in range(2):
        X[h, 0, rows(c, z), cols(x)] = tok_ref[h * hr:(h + 1) * hr, :]
        X[h, 1, rows(c, z), cols(x)] = cot_ref[h * hr:(h + 1) * hr, :]
    full = 2 * hr
    lane = lax.broadcasted_iota(jnp.int32, (full, LANES), 1)
    sub = lax.broadcasted_iota(jnp.int32, (full, LANES), 0)
    weights = scale_ref[...].astype(jnp.float32) / 4096.0
    routes = routes_ref[...]

    for expert in range(ep):
        column = jnp.sum(jnp.where(routes == expert, weights, 0.0), axis=1, keepdims=True)
        row = jnp.sum(jnp.where(lane == sub, column, 0.0), axis=0, keepdims=True)
        WS[expert] = jnp.broadcast_to(row, (8, LANES))

    barrier = pltpu.get_barrier_semaphore()

    def greet(d, carry):
        other = lax.rem(me + d, n)
        pl.semaphore_signal(
            barrier, inc=1, device_id=(g, lax.div(other, nx), lax.rem(other, nx)), device_id_type=MESH
        )
        return carry

    lax.fori_loop(1, n, greet, 0)
    acc[...] = jnp.zeros_like(acc)
    rp[...] = jnp.zeros_like(rp)
    pl.semaphore_wait(barrier, n - 1)

    def zcopy(h, zb, way):
        part = X.at[h, :, rows(c, zb), cols(x)]
        to = z + 1 if way == 0 else z - 1
        return remote(part, part, zs.at[h, zb, way], zr.at[h, zb], (g, 2 * to + c, x))

    def xcopy(h, zb, d):
        part = X.at[h, :, rows(c, zb), cols(x)]
        return remote(part, part, xs.at[h, d, zb], xr.at[h, d, zb], (g, e, lax.rem(x + d, nx)))

    def xarrival(h, zb, d):
        part = X.at[h, :, rows(c, zb), cols(lax.rem(x - d + nx, nx))]
        return remote(part, part, xs.at[h, d, zb], xr.at[h, d, zb], (g, e, lax.rem(x + d, nx)))

    def ccopy(h, zb, xb):
        part = X.at[h, :, rows(c, zb), cols(xb)]
        return remote(part, part, cs.at[h, xb, zb], cr.at[h, xb, zb], (g, 2 * z + 1 - c, x))

    def carrival(h, zb, xb):
        part = X.at[h, :, rows(1 - c, zb), cols(xb)]
        return remote(part, part, cs.at[h, xb, zb], cr.at[h, xb, zb], (g, 2 * z + 1 - c, x))

    def spread(h, zb):
        for d in range(1, nx):
            xcopy(h, zb, d).start()
        ccopy(h, zb, x).start()

    def own(h):
        @pl.when(z < nz - 1)
        def _():
            zcopy(h, z, 0).start()

        @pl.when(z > 0)
        def _():
            zcopy(h, z, 1).start()

        spread(h, z)

    def step(h, s):
        @pl.when(z - s >= 0)
        def _():
            zcopy(h, z - s, 0).wait_recv()

            @pl.when(z < nz - 1)
            def _():
                zcopy(h, z - s, 0).start()

            spread(h, z - s)

        @pl.when(z + s < nz)
        def _():
            zcopy(h, z + s, 1).wait_recv()

            @pl.when(z > 0)
            def _():
                zcopy(h, z + s, 1).start()

            spread(h, z + s)

    def at_distance(s, fn):
        if s == 0:
            fn(z)
            return

        @pl.when(z - s >= 0)
        def _():
            fn(z - s)

        @pl.when(z + s < nz)
        def _():
            fn(z + s)

    def xwait(h, s):
        def one(zb):
            for d in range(1, nx):
                xarrival(h, zb, d).wait_recv()
                ccopy(h, zb, lax.rem(x - d + nx, nx)).start()

        at_distance(s, one)

    def cwait(h):
        for zb in range(nz):
            for xb in range(nx):
                carrival(h, zb, xb).wait_recv()

    def drain_gather(h):
        for zb in range(nz):
            @pl.when(jnp.logical_and(zb <= z, z < nz - 1))
            def _():
                zcopy(h, zb, 0).wait_send()

            @pl.when(jnp.logical_and(zb >= z, z > 0))
            def _():
                zcopy(h, zb, 1).wait_send()

            for d in range(1, nx):
                xcopy(h, zb, d).wait_send()
            for xb in range(nx):
                ccopy(h, zb, xb).wait_send()

    def bcopy(d):
        to = lax.rem(e + d, ep)
        return remote(WS.at[to], WR.at[e], bs.at[to], br.at[e], (g, to, x))

    def barrival(d):
        frm = lax.rem(e - d + ep, ep)
        return remote(WS.at[frm], WR.at[frm], bs.at[frm], br.at[frm], (g, frm, x))

    own(0)
    lax.fori_loop(1, ep, lambda d, carry: (bcopy(d).start(), carry)[1], 0)
    for s in range(1, nz):
        step(0, s)
        xwait(0, s - 1)
    own(1)
    xwait(0, nz - 1)
    lax.fori_loop(1, ep, lambda d, carry: (barrival(d).wait_recv(), carry)[1], 0)
    WR[e] = WS[e]
    hlane = lax.broadcasted_iota(jnp.int32, (hr, LANES), 1)
    hsub = lax.broadcasted_iota(jnp.int32, (hr, LANES), 0)
    for cc in range(2):
        for zz in range(nz):
            row = WR[2 * zz + cc][0:1, :]
            for h in range(2):
                column = jnp.sum(jnp.where(hlane == hsub + h * hr, row, 0.0), axis=1, keepdims=True)
                q = (cc * nz + zz) * hr
                wv[h, q:q + hr, :] = jnp.broadcast_to(column, (hr, LANES))
    cwait(0)

    def core_copy(h):
        return remote(SC.at[h], RC.at[h], ccs.at[h], ccr.at[h], (g, 2 * z + 1 - c, x))

    def cx_copy(h, d):
        return remote(SX.at[h, d - 1], RX.at[h, d - 1], cxs.at[h, d], cxr.at[h, d], (g, e, lax.rem(x + d, nx)))

    def cz_copy(h, d):
        to = lax.rem(z + d, nz)
        part = SZ.at[h, pl.ds(pl.multiple_of(to * hr, hr), hr), :]
        return remote(part, RZ.at[h, d - 1], czs.at[h, d], czr.at[h, d], (g, 2 * to + c, x))

    def stage_core(h):
        SC[h] = acc[h, rows(1 - c, 0, nz), :].astype(jnp.bfloat16)
        core_copy(h).start()

    def stage_x(h):
        core_copy(h).wait_recv()
        for d in range(1, nx):
            there = cols(lax.rem(x + d, nx))
            SX[h, d - 1] = (
                acc[h, rows(c, 0, nz), there] + RC[h, :, there].astype(jnp.float32)
            ).astype(jnp.bfloat16)
            cx_copy(h, d).start()
        S2[h] = acc[h, rows(c, 0, nz), cols(x)] + RC[h, :, cols(x)].astype(jnp.float32)

    def stage_z(h):
        total = S2[h]
        for d in range(1, nx):
            cx_copy(h, d).wait_recv()
            total = total + RX[h, d - 1].astype(jnp.float32)
        S2[h] = total
        SZ[h] = total.astype(jnp.bfloat16)
        for d in range(1, nz):
            cz_copy(h, d).start()

    def stage_out(h):
        total = S2[h, pl.ds(pl.multiple_of(z * hr, hr), hr), :]
        for d in range(1, nz):
            cz_copy(h, d).wait_recv()
            total = total + RZ[h, d - 1].astype(jnp.float32)
        out_ref[h * hr:(h + 1) * hr, :] = total.astype(jnp.bfloat16)

    def compute(h, slot, w):
        gate = jnp.dot(X[h, 0], Wg[slot, :, 0:w], preferred_element_type=jnp.float32)
        up = jnp.dot(X[h, 0], Wu[slot, :, 0:w], preferred_element_type=jnp.float32)
        back = contract_last(X[h, 1], Wd[slot, 0:w, :])
        sig = jax.nn.sigmoid(gate)
        act = gate * sig
        rp[h] += jnp.sum(act * up * back, axis=1, keepdims=True)
        scaled = wv[h][:, 0:1] * back
        up_grad = (scaled * act).astype(jnp.bfloat16)
        gate_grad = (scaled * up * sig * (1.0 + gate * (1.0 - sig))).astype(jnp.bfloat16)
        depth = acc.shape[2]
        chunk = 512 if depth % 512 == 0 else LANES

        def part(j, carry):
            at = pl.ds(pl.multiple_of(j * chunk, chunk), chunk)
            acc[h, :, at] += contract_last(gate_grad, Wg[slot, at, 0:w]) + contract_last(
                up_grad, Wu[slot, at, 0:w]
            )
            return carry

        lax.fori_loop(0, depth // chunk, part, 0)

    events = {}

    def plan(i, fn):
        events.setdefault(i, []).append(fn)

    for s in range(1, nz + 1):
        def event(s=s):
            if s < nz:
                step(1, s)
            xwait(1, s - 1)

        plan(min(s, nt - 1), event)
    plan(nt, lambda: cwait(1))
    plan(nt, lambda: stage_core(0))
    plan(min(nt + 1, 2 * nt - 1), lambda: stage_x(0))
    plan(min(nt + 3, 2 * nt - 1), lambda: stage_z(0))

    def iteration(i, carry):
        h = lax.div(i, nt)
        t = lax.rem(i, nt)
        slot = lax.rem(i, 2) if nt > 1 else 0
        for at in sorted(events):
            @pl.when(i == at)
            def _():
                for fn in events[at]:
                    fn()

        if nt == 1:
            @pl.when(i == 0)
            def _():
                for copy in tile_copies(0, 0):
                    copy.wait()

            compute(h, 0, widths[0])
            return carry

        following = lax.rem(t + 1, nt)
        other = 1 - slot

        @pl.when(jnp.logical_and(i + 1 < 2 * nt, following < nt - 1))
        def _():
            for copy in main_copies(following, other):
                copy.start()

        @pl.when(jnp.logical_and(i + 1 < 2 * nt, following == nt - 1))
        def _():
            for copy in tile_copies(nt - 1, other):
                copy.start()

        @pl.when(t < nt - 1)
        def _():
            for copy in main_copies(t, slot):
                copy.wait()
            compute(h, slot, widths[0])

        @pl.when(t == nt - 1)
        def _():
            for copy in tile_copies(nt - 1, slot):
                copy.wait()
            compute(h, slot, widths[nt - 1])

        return carry

    lax.fori_loop(0, 2 * nt, iteration, 0)

    stage_core(1)
    for cc in range(2):
        for zz in range(nz):
            q = (cc * nz + zz) * hr
            row = jnp.zeros((1, LANES), jnp.float32)
            for h in range(2):
                row = row + jnp.sum(
                    jnp.where(hlane == hsub + h * hr, rp[h, q:q + hr, :], 0.0), axis=0, keepdims=True
                )
            RS[2 * zz + cc] = jnp.broadcast_to(row, (8, LANES))

    def pcopy(d):
        other = lax.rem(me + d, n)
        oe, ox = lax.div(other, nx), lax.rem(other, nx)
        return remote(RS.at[oe], RR.at[me], ps.at[other], pr.at[me], (g, oe, ox))

    def parrival(d):
        frm = lax.rem(me - d + n, n)
        fe, fx = lax.div(frm, nx), lax.rem(frm, nx)
        return remote(RS.at[fe], RR.at[frm], ps.at[frm], pr.at[frm], (g, fe, fx))

    lax.fori_loop(1, n, lambda d, carry: (pcopy(d).start(), carry)[1], 0)
    stage_x(1)
    stage_out(0)
    stage_z(1)
    lax.fori_loop(1, n, lambda d, carry: (parrival(d).wait_recv(), carry)[1], 0)
    RR[me] = RS[e]
    grad = jnp.zeros(routes.shape, jnp.float32)
    for expert in range(ep):
        row = jnp.zeros((1, LANES), jnp.float32)
        for xx in range(nx):
            row = row + RR[expert * nx + xx][0:1, :]
        column = jnp.sum(jnp.where(lane == sub, row, 0.0), axis=1, keepdims=True)
        grad = grad + jnp.where(routes == expert, column, 0.0)
    rg_ref[...] = grad * (1.0 / math.sqrt(FF))
    stage_out(1)

    for h in range(2):
        drain_gather(h)
        core_copy(h).wait_send()
        for d in range(1, nx):
            cx_copy(h, d).wait_send()
        for d in range(1, nz):
            cz_copy(h, d).wait_send()
    lax.fori_loop(1, ep, lambda d, carry: (bcopy(d).wait_send(), carry)[1], 0)
    lax.fori_loop(1, n, lambda d, carry: (pcopy(d).wait_send(), carry)[1], 0)


def shards(tokens, cotangent, routes, route_scale, gate_weight, up_weight, down_weight):
    ep, nx = lax.axis_size("ep"), lax.axis_size("fsdp")
    nz = ep // 2
    n = ep * nx
    block, dx = tokens.shape
    hr = block // 2
    depth, hidden = gate_weight.shape[1:]
    half = ep * hr
    mine = nz * hr
    if hidden % LANES == 0 and hidden > TILE:
        widths = [TILE] * (hidden // TILE) + ([hidden % TILE] if hidden % TILE else [])
    else:
        widths = [hidden]
    slots = min(2, len(widths))
    bf16, f32 = jnp.bfloat16, jnp.float32
    dma = pltpu.SemaphoreType.DMA
    vmem = pl.BlockSpec(memory_space=pltpu.VMEM)
    return pl.pallas_call(
        functools.partial(kernel, nz, nx, widths),
        out_shape=(
            jax.ShapeDtypeStruct((block, dx), bf16),
            jax.ShapeDtypeStruct(routes.shape, f32),
        ),
        in_specs=[vmem] * 4 + [pl.BlockSpec(memory_space=pl.ANY)] * 3,
        out_specs=(vmem, vmem),
        scratch_shapes=[
            pltpu.VMEM((2, 2, half, depth), bf16),
            pltpu.VMEM((slots, depth, widths[0]), bf16),
            pltpu.VMEM((slots, depth, widths[0]), bf16),
            pltpu.VMEM((slots, widths[0], depth), bf16),
            pltpu.VMEM((2, half, depth), f32),
            pltpu.VMEM((2, half, LANES), f32),
            pltpu.VMEM((2, half, LANES), f32),
            pltpu.VMEM((ep, 8, LANES), f32),
            pltpu.VMEM((ep, 8, LANES), f32),
            pltpu.VMEM((ep, 8, LANES), f32),
            pltpu.VMEM((n, 8, LANES), f32),
            pltpu.VMEM((2, mine, depth), bf16),
            pltpu.VMEM((2, mine, depth), bf16),
            pltpu.VMEM((2, nx - 1, mine, dx), bf16),
            pltpu.VMEM((2, nx - 1, mine, dx), bf16),
            pltpu.VMEM((2, mine, dx), f32),
            pltpu.VMEM((2, mine, dx), bf16),
            pltpu.VMEM((2, nz - 1, hr, dx), bf16),
            dma((slots, 3)),
            dma((2, nz, 2)),
            dma((2, nz)),
            dma((2, nx, nz)),
            dma((2, nx, nz)),
            dma((2, nx, nz)),
            dma((2, nx, nz)),
            dma((ep,)),
            dma((ep,)),
            dma((n,)),
            dma((n,)),
            dma((2,)),
            dma((2,)),
            dma((2, nx)),
            dma((2, nx)),
            dma((2, nz)),
            dma((2, nz)),
        ],
        compiler_params=pltpu.CompilerParams(
            collective_id=0, has_side_effects=True, vmem_limit_bytes=62 * 1024 * 1024
        ),
        cost_estimate=pl.CostEstimate(
            flops=20 * half * depth * hidden, bytes_accessed=12 * depth * hidden, transcendentals=0
        ),
    )(tokens, cotangent, routes, route_scale, gate_weight, up_weight, down_weight)


def solution(mesh):
    in_specs = (
        P(("groups", "ep"), "fsdp"),
        P(("groups", "ep"), "fsdp"),
        P(("groups", "ep"), None),
        P(("groups", "ep"), None),
        P("ep", None, "fsdp"),
        P("ep", None, "fsdp"),
        P("ep", "fsdp", None),
    )
    out_specs = (P(("groups", "ep"), "fsdp"), P(("groups", "ep"), None))
    return jax.shard_map(shards, mesh=mesh, in_specs=in_specs, out_specs=out_specs, check_vma=False)
```

time: 342 us -> 127 us (0.37)
  waiting for transfers between devices: 142 us -> 0 us
  Pallas kernels: 0 us -> 121 us
  matrix products: 99.3 us -> 0 us
  blocking collectives: 49.2 us -> 0 us
  local copies, waits for them, and re-layouts: 33.7 us -> 5.79 us
  between operations: 13.9 us -> 0.64 us
  other arithmetic: 3.96 us -> 0 us
    pallas_call x0 -> x1, Pallas kernels: none -> 121 us  [shards(): pl.pallas_call(functools.partial(kernel, nz, nx, widths), out_shape=(jax....]
    reduce_scatter x2 -> x0, waiting for transfers between devices: 115 us -> none  [the longest x1 75.4 us: shards(): lax.psum_scatter(partial_value, 'fsdp', scatter_dimension=1, tiled=True)]
    dot_general x5 -> x0, matrix products: 99.3 us -> none  [the longest x3 68.9 us: contract_last(): lax.dot_general(left, right, (((1,), (1,)), ((), ())), preferred_element_...]
    all_gather x4 -> x0, blocking collectives: 44.2 us -> none  [the longest x1 13.7 us: shards(): lax.all_gather(routes, 'ep', axis=0, tiled=True)]
    gather x4 -> x0, local copies, waits for them, and re-layouts: 26 us -> none  [the longest x1 8.58 us: shards(): tile_cot = all_cot[source]]
    unnamed x6 -> x0, waiting for transfers between devices: 25.2 us -> none
    psum x1 -> x0, blocking collectives: 4.92 us -> none  [shards(): route_tile = lax.psum(route_part, 'fsdp')]
    scatter x2 -> x0, local copies, waits for them, and re-layouts: 4.87 us -> none  [the longest x1 2.44 us: shards(): jnp.zeros((capacity,), jnp.int32).at[slot_index].set(positions, mode='drop')]
  transfers between devices with their start and end apart: 5 -> 0, of which waited for: 5 -> 0; matrix products, arithmetic and copies ran while one was open for 15% -> 0% of each run, Pallas kernels for 0% -> 0%
where the time goes in v1:
time: 127 us
  Pallas kernels  121 us (95%)
  local copies, waits for them, and re-layouts  5.79 us (5%)
    pallas_call x1, Pallas kernels, shards(): pl.pallas_call(functools.partial(kernel, nz, nx, widths), out_shape=(jax....  121 us
    unnamed x3, local copies, waits for them, and re-layouts  4.38 us

profile of v1, /device:TPU:0, one launch (start us, length us, event | category | flops | bytes accessed | tf_op | source)
XLA Modules:
  0.0 127.0 jit_solution(9096572287433294576)
XLA Ops:
  0.6 1.4 %copy.9.routes_ref = s32[64,4]{1,0:T(8,128)} copy(s32[64,4]{0,1:T(4,128)} %param.9) | data formatting | bytes 2048 | tf_op args[2]
  2.0 1.4 %copy.10.scale_ref = s32[64,4]{1,0:T(8,128)} copy(s32[64,4]{0,1:T(4,128)} %param.10) | data formatting | bytes 2048 | tf_op args[3]
  3.4 120.6 %shard_map.86 = (bf16[64,1536]{1,0:T(8,128)(2,1)}, f32[64,4]{1,0:T(8,128)}) custom-call(bf16[64,1536]{1,0:T(8,128)(2,1)} %tok_ref.1, bf16[64,1536]{1,0:T(8,128)(2,1)} %cot_ref.1, s32[64,4]{1,0:T(8,128)} %copy.9.routes_ref, s32[64,4]{1,0:T(8,128)} %copy.10.scale_ref, bf16[1,3072,2688]{2,1,0:T(8,128)(2,1)} %wg_hbm.1, bf16[1,3072,2688]{2,1,0:T(8,128)(2,1)} %wu_hbm.1, ...), custom_call_target="tpu_custom_call" | custom-call | flops 42278584320 | bytes 99090432 | tf_op jit(solution)/shard_map/pallas_call | solution.py:422
  124.0 1.4 %copy.11 = f32[64,4]{0,1:T(4,128)} copy(f32[64,4]{1,0:T(8,128)} %get-tuple-element.3) | data formatting | bytes 2048 | tf_op jit(solution)/shard_map/pallas_call | solution.py:422
  125.4 1.6 %copy.13 = bf16[64,1536]{1,0:T(8,128)(2,1)} copy(bf16[64,1536]{1,0:T(8,128)(2,1)} %get-tuple-element.6) | data formatting | bytes 393216

commit v2 on v1

--- a/solution.py
+++ b/solution.py
@@ -23,8 +23,8 @@
 def kernel(
     nz, nx, widths, tok_ref, cot_ref, routes_ref, scale_ref, wg_hbm, wu_hbm, wd_hbm,
     out_ref, rg_ref,
-    X, Wg, Wu, Wd, acc, rp, wv, WS, WR, RS, RR, SC, RC, SX, RX, S2, SZ, RZ,
-    wsem, zs, zr, xs, xr, cs, cr, bs, br, ps, pr, ccs, ccr, cxs, cxr, czs, czr,
+    X, Wg, Wu, Wd, Vg, Vu, GG, UG, acc, rp, wv, WS, WR, RS, RR, SC, RC, SX, RX, S2, SZ, RZ,
+    wsem, vsem, zs, zr, xs, xr, cs, cr, bs, br, ps, pr, ccs, ccr, cxs, cxr, czs, czr,
 ):
     ep = 2 * nz
     n = ep * nx
@@ -32,6 +32,10 @@
     dx = tok_ref.shape[1]
     hr = tok_ref.shape[0] // 2
     mine = nz * hr
+    half = 2 * mine
+    cw = acc.shape[2]
+    kc = dx // cw
+    steps = kc * nx
     g = lax.axis_index("groups")
     e = lax.axis_index("ep")
     x = lax.axis_index("fsdp")
@@ -94,7 +98,6 @@
         return carry
 
     lax.fori_loop(1, n, greet, 0)
-    acc[...] = jnp.zeros_like(acc)
     rp[...] = jnp.zeros_like(rp)
     pl.semaphore_wait(barrier, n - 1)
 
@@ -225,49 +228,58 @@
                 wv[h, q:q + hr, :] = jnp.broadcast_to(column, (hr, LANES))
     cwait(0)
 
-    def core_copy(h):
-        return remote(SC.at[h], RC.at[h], ccs.at[h], ccr.at[h], (g, 2 * z + 1 - c, x))
-
-    def cx_copy(h, d):
-        return remote(SX.at[h, d - 1], RX.at[h, d - 1], cxs.at[h, d], cxr.at[h, d], (g, e, lax.rem(x + d, nx)))
-
-    def cz_copy(h, d):
+    def chunk_copies(k, slot):
+        to = lax.rem(x + 1 + lax.div(k, kc), nx)
+        at = pl.ds(pl.multiple_of(to * dx + lax.rem(k, kc) * cw, LANES), cw)
+        return (
+            pltpu.make_async_copy(wg_hbm.at[0, at, :], Vg.at[slot], vsem.at[slot, 0]),
+            pltpu.make_async_copy(wu_hbm.at[0, at, :], Vu.at[slot], vsem.at[slot, 1]),
+        )
+
+    def core_copy(k):
+        return remote(SC.at[k], RC.at[k], ccs.at[k], ccr.at[k], (g, 2 * z + 1 - c, x))
+
+    def cx_copy(k):
+        return remote(SX.at[k], RX.at[k], cxs.at[k], cxr.at[k], (g, e, lax.rem(x + 1 + k // kc, nx)))
+
+    def cz_copy(j, d):
         to = lax.rem(z + d, nz)
-        part = SZ.at[h, pl.ds(pl.multiple_of(to * hr, hr), hr), :]
-        return remote(part, RZ.at[h, d - 1], czs.at[h, d], czr.at[h, d], (g, 2 * to + c, x))
-
-    def stage_core(h):
-        SC[h] = acc[h, rows(1 - c, 0, nz), :].astype(jnp.bfloat16)
-        core_copy(h).start()
-
-    def stage_x(h):
-        core_copy(h).wait_recv()
-        for d in range(1, nx):
-            there = cols(lax.rem(x + d, nx))
-            SX[h, d - 1] = (
-                acc[h, rows(c, 0, nz), there] + RC[h, :, there].astype(jnp.float32)
-            ).astype(jnp.bfloat16)
-            cx_copy(h, d).start()
-        S2[h] = acc[h, rows(c, 0, nz), cols(x)] + RC[h, :, cols(x)].astype(jnp.float32)
-
-    def stage_z(h):
-        total = S2[h]
-        for d in range(1, nx):
-            cx_copy(h, d).wait_recv()
-            total = total + RX[h, d - 1].astype(jnp.float32)
-        S2[h] = total
-        SZ[h] = total.astype(jnp.bfloat16)
+        part = SZ.at[j, :, pl.ds(pl.multiple_of(to * hr, hr), hr), :]
+        return remote(part, RZ.at[j, d - 1], czs.at[j, d], czr.at[j, d], (g, 2 * to + c, x))
+
+    def piece(slot, h, cc):
+        return acc[slot, pl.ds(pl.multiple_of(h * half + cc * mine, mine), mine), :]
+
+    def stage_x(k):
+        core_copy(k).wait_recv()
+        for h in range(2):
+            SX[k, h] = (piece(k % 2, h, c) + RC[k, h].astype(jnp.float32)).astype(jnp.bfloat16)
+        cx_copy(k).start()
+
+    def stage_z(k):
+        j = k % kc
+        core_copy(k).wait_recv()
+        for d in range(nx - 1):
+            cx_copy(d * kc + j).wait_recv()
+        for h in range(2):
+            total = piece(k % 2, h, c) + RC[k, h].astype(jnp.float32)
+            for d in range(nx - 1):
+                total = total + RX[d * kc + j, h].astype(jnp.float32)
+            S2[j, h] = total
+            SZ[j, h] = total.astype(jnp.bfloat16)
         for d in range(1, nz):
-            cz_copy(h, d).start()
-
-    def stage_out(h):
-        total = S2[h, pl.ds(pl.multiple_of(z * hr, hr), hr), :]
+            cz_copy(j, d).start()
+
+    def stage_out(j):
         for d in range(1, nz):
-            cz_copy(h, d).wait_recv()
-            total = total + RZ[h, d - 1].astype(jnp.float32)
-        out_ref[h * hr:(h + 1) * hr, :] = total.astype(jnp.bfloat16)
-
-    def compute(h, slot, w):
+            cz_copy(j, d).wait_recv()
+        for h in range(2):
+            total = S2[j, h, pl.ds(pl.multiple_of(z * hr, hr), hr), :]
+            for d in range(1, nz):
+                total = total + RZ[j, d - 1, h].astype(jnp.float32)
+            out_ref[h * hr:(h + 1) * hr, j * cw:(j + 1) * cw] = total.astype(jnp.bfloat16)
+
+    def compute(h, slot, w, off):
         gate = jnp.dot(X[h, 0], Wg[slot, :, 0:w], preferred_element_type=jnp.float32)
         up = jnp.dot(X[h, 0], Wu[slot, :, 0:w], preferred_element_type=jnp.float32)
         back = contract_last(X[h, 1], Wd[slot, 0:w, :])
@@ -275,19 +287,9 @@
         act = gate * sig
         rp[h] += jnp.sum(act * up * back, axis=1, keepdims=True)
         scaled = wv[h][:, 0:1] * back
-        up_grad = (scaled * act).astype(jnp.bfloat16)
-        gate_grad = (scaled * up * sig * (1.0 + gate * (1.0 - sig))).astype(jnp.bfloat16)
-        depth = acc.shape[2]
-        chunk = 512 if depth % 512 == 0 else LANES
-
-        def part(j, carry):
-            at = pl.ds(pl.multiple_of(j * chunk, chunk), chunk)
-            acc[h, :, at] += contract_last(gate_grad, Wg[slot, at, 0:w]) + contract_last(
-                up_grad, Wu[slot, at, 0:w]
-            )
-            return carry
-
-        lax.fori_loop(0, depth // chunk, part, 0)
+        here = pl.ds(pl.multiple_of(h * half, half), half)
+        UG[here, pl.ds(off, w)] = (scaled * act).astype(jnp.bfloat16)
+        GG[here, pl.ds(off, w)] = (scaled * up * sig * (1.0 + gate * (1.0 - sig))).astype(jnp.bfloat16)
 
     events = {}
 
@@ -302,9 +304,13 @@
 
         plan(min(s, nt - 1), event)
     plan(nt, lambda: cwait(1))
-    plan(nt, lambda: stage_core(0))
-    plan(min(nt + 1, 2 * nt - 1), lambda: stage_x(0))
-    plan(min(nt + 3, 2 * nt - 1), lambda: stage_z(0))
+
+    def first_chunks():
+        for k in range(min(2, steps)):
+            for copy in chunk_copies(k, k):
+                copy.start()
+
+    plan(nt, first_chunks)
 
     def iteration(i, carry):
         h = lax.div(i, nt)
@@ -322,7 +328,7 @@
                 for copy in tile_copies(0, 0):
                     copy.wait()
 
-            compute(h, 0, widths[0])
+            compute(h, 0, widths[0], 0)
             return carry
 
         following = lax.rem(t + 1, nt)
@@ -342,19 +348,18 @@
         def _():
             for copy in main_copies(t, slot):
                 copy.wait()
-            compute(h, slot, widths[0])
+            compute(h, slot, widths[0], pl.multiple_of(t * widths[0], widths[0]))
 
         @pl.when(t == nt - 1)
         def _():
             for copy in tile_copies(nt - 1, slot):
                 copy.wait()
-            compute(h, slot, widths[nt - 1])
+            compute(h, slot, widths[nt - 1], sum(widths[:nt - 1]))
 
         return carry
 
     lax.fori_loop(0, 2 * nt, iteration, 0)
 
-    stage_core(1)
     for cc in range(2):
         for zz in range(nz):
             q = (cc * nz + zz) * hr
@@ -376,11 +381,38 @@
         return remote(RS.at[fe], RR.at[frm], ps.at[frm], pr.at[frm], (g, fe, fx))
 
     lax.fori_loop(1, n, lambda d, carry: (pcopy(d).start(), carry)[1], 0)
-    stage_x(1)
-    stage_out(0)
-    stage_z(1)
+
+    def after(k):
+        if k // kc < nx - 1:
+            stage_x(k)
+        else:
+            stage_z(k)
+
+    def back_step(k, carry):
+        slot = lax.rem(k, 2)
+        for copy in chunk_copies(k, slot):
+            copy.wait()
+        acc[slot] = contract_last(GG[...], Vg[slot]) + contract_last(UG[...], Vu[slot])
+        for h in range(2):
+            SC[k, h] = piece(slot, h, 1 - c).astype(jnp.bfloat16)
+        core_copy(k).start()
+
+        @pl.when(k + 2 < steps)
+        def _():
+            for copy in chunk_copies(k + 2, slot):
+                copy.start()
+
+        for done in range(steps - 1):
+            @pl.when(k == done + 1)
+            def _():
+                after(done)
+
+        return carry
+
+    lax.fori_loop(0, steps, back_step, 0)
     lax.fori_loop(1, n, lambda d, carry: (parrival(d).wait_recv(), carry)[1], 0)
     RR[me] = RS[e]
+    after(steps - 1)
     grad = jnp.zeros(routes.shape, jnp.float32)
     for expert in range(ep):
         row = jnp.zeros((1, LANES), jnp.float32)
@@ -389,17 +421,19 @@
         column = jnp.sum(jnp.where(lane == sub, row, 0.0), axis=1, keepdims=True)
         grad = grad + jnp.where(routes == expert, column, 0.0)
     rg_ref[...] = grad * (1.0 / math.sqrt(FF))
-    stage_out(1)
 
     for h in range(2):
         drain_gather(h)
-        core_copy(h).wait_send()
-        for d in range(1, nx):
-            cx_copy(h, d).wait_send()
-        for d in range(1, nz):
-            cz_copy(h, d).wait_send()
+    for k in range(steps):
+        core_copy(k).wait_send()
+    for k in range(steps - kc):
+        cx_copy(k).wait_send()
     lax.fori_loop(1, ep, lambda d, carry: (bcopy(d).wait_send(), carry)[1], 0)
     lax.fori_loop(1, n, lambda d, carry: (pcopy(d).wait_send(), carry)[1], 0)
+    for j in range(kc):
+        stage_out(j)
+        for d in range(1, nz):
+            cz_copy(j, d).wait_send()
 
 
 def shards(tokens, cotangent, routes, route_scale, gate_weight, up_weight, down_weight):
@@ -416,6 +450,9 @@
     else:
         widths = [hidden]
     slots = min(2, len(widths))
+    cw = TILE if dx % TILE == 0 else dx
+    kc = dx // cw
+    steps = kc * nx
     bf16, f32 = jnp.bfloat16, jnp.float32
     dma = pltpu.SemaphoreType.DMA
     vmem = pl.BlockSpec(memory_space=pltpu.VMEM)
@@ -432,21 +469,26 @@
             pltpu.VMEM((slots, depth, widths[0]), bf16),
             pltpu.VMEM((slots, depth, widths[0]), bf16),
             pltpu.VMEM((slots, widths[0], depth), bf16),
-            pltpu.VMEM((2, half, depth), f32),
+            pltpu.VMEM((2, cw, hidden), bf16),
+            pltpu.VMEM((2, cw, hidden), bf16),
+            pltpu.VMEM((2 * half, hidden), bf16),
+            pltpu.VMEM((2 * half, hidden), bf16),
+            pltpu.VMEM((2, 2 * half, cw), f32),
             pltpu.VMEM((2, half, LANES), f32),
             pltpu.VMEM((2, half, LANES), f32),
             pltpu.VMEM((ep, 8, LANES), f32),
             pltpu.VMEM((ep, 8, LANES), f32),
             pltpu.VMEM((ep, 8, LANES), f32),
             pltpu.VMEM((n, 8, LANES), f32),
-            pltpu.VMEM((2, mine, depth), bf16),
-            pltpu.VMEM((2, mine, depth), bf16),
-            pltpu.VMEM((2, nx - 1, mine, dx), bf16),
-            pltpu.VMEM((2, nx - 1, mine, dx), bf16),
-            pltpu.VMEM((2, mine, dx), f32),
-            pltpu.VMEM((2, mine, dx), bf16),
-            pltpu.VMEM((2, nz - 1, hr, dx), bf16),
+            pltpu.VMEM((steps, 2, mine, cw), bf16),
+            pltpu.VMEM((steps, 2, mine, cw), bf16),
+            pltpu.VMEM((steps - kc, 2, mine, cw), bf16),
+            pltpu.VMEM((steps - kc, 2, mine, cw), bf16),
+            pltpu.VMEM((kc, 2, mine, cw), f32),
+            pltpu.VMEM((kc, 2, mine, cw), bf16),
+            pltpu.VMEM((kc, nz - 1, 2, hr, cw), bf16),
             dma((slots, 3)),
+            dma((2, 2)),
             dma((2, nz, 2)),
             dma((2, nz)),
             dma((2, nx, nz)),
@@ -457,12 +499,12 @@
             dma((ep,)),
             dma((n,)),
             dma((n,)),
-            dma((2,)),
-            dma((2,)),
-            dma((2, nx)),
-            dma((2, nx)),
-            dma((2, nz)),
-            dma((2, nz)),
+            dma((steps,)),
+            dma((steps,)),
+            dma((steps,)),
+            dma((steps,)),
+            dma((kc, nz)),
+            dma((kc, nz)),
         ],
         compiler_params=pltpu.CompilerParams(
             collective_id=0, has_side_effects=True, vmem_limit_bytes=62 * 1024 * 1024

time: 127 us -> 119 us (0.937)
  Pallas kernels: 121 us -> 113 us
    pallas_call x1, Pallas kernels: 121 us -> 113 us  [shards(): pl.pallas_call(functools.partial(kernel, nz, nx, widths), out_shape=(jax....]
where the time goes in v2:
time: 119 us
  Pallas kernels  113 us (95%)
  local copies, waits for them, and re-layouts  5.79 us (5%)
    pallas_call x1, Pallas kernels, shards(): pl.pallas_call(functools.partial(kernel, nz, nx, widths), out_shape=(jax....  113 us
    unnamed x3, local copies, waits for them, and re-layouts  4.38 us

profile of v2, /device:TPU:0, one launch (start us, length us, event | category | flops | bytes accessed | tf_op | source)
XLA Modules:
  0.0 119.2 jit_solution(17475998304517765304)
XLA Ops:
  0.6 1.4 %copy.9.routes_ref = s32[64,4]{1,0:T(8,128)} copy(s32[64,4]{0,1:T(4,128)} %param.9) | data formatting | bytes 2048 | tf_op args[2]
  2.0 1.4 %copy.10.scale_ref = s32[64,4]{1,0:T(8,128)} copy(s32[64,4]{0,1:T(4,128)} %param.10) | data formatting | bytes 2048 | tf_op args[3]
  3.4 112.8 %shard_map.86 = (bf16[64,1536]{1,0:T(8,128)(2,1)}, f32[64,4]{1,0:T(8,128)}) custom-call(bf16[64,1536]{1,0:T(8,128)(2,1)} %tok_ref.1, bf16[64,1536]{1,0:T(8,128)(2,1)} %cot_ref.1, s32[64,4]{1,0:T(8,128)} %copy.9.routes_ref, s32[64,4]{1,0:T(8,128)} %copy.10.scale_ref, bf16[1,3072,2688]{2,1,0:T(8,128)(2,1)} %wg_hbm.1, bf16[1,3072,2688]{2,1,0:T(8,128)(2,1)} %wu_hbm.1, ...), custom_call_target="tpu_custom_call" | custom-call | flops 42278584320 | bytes 99090432 | tf_op jit(solution)/shard_map/pallas_call | solution.py:459
  116.2 1.4 %copy.11 = f32[64,4]{0,1:T(4,128)} copy(f32[64,4]{1,0:T(8,128)} %get-tuple-element.3) | data formatting | bytes 2048 | tf_op jit(solution)/shard_map/pallas_call | solution.py:459
  117.6 1.6 %copy.13 = bf16[64,1536]{1,0:T(8,128)(2,1)} copy(bf16[64,1536]{1,0:T(8,128)(2,1)} %get-tuple-element.6) | data formatting | bytes 393216

commit v3 on v2

--- a/solution.py
+++ b/solution.py
@@ -12,6 +12,7 @@
 MESH = pl.DeviceIdType.MESH
 LANES = 128
 TILE = 512
+CHUNK = 256
 
 
 def contract_last(left, right):
@@ -71,23 +72,6 @@
             pltpu.make_async_copy(wd_hbm.at[0, pl.ds(off, w), :], Wd.at[slot, pl.ds(0, w), :], wsem.at[slot, 2]),
         )
 
-    for copy in tile_copies(0, 0):
-        copy.start()
-
-    for h in range(2):
-        X[h, 0, rows(c, z), cols(x)] = tok_ref[h * hr:(h + 1) * hr, :]
-        X[h, 1, rows(c, z), cols(x)] = cot_ref[h * hr:(h + 1) * hr, :]
-    full = 2 * hr
-    lane = lax.broadcasted_iota(jnp.int32, (full, LANES), 1)
-    sub = lax.broadcasted_iota(jnp.int32, (full, LANES), 0)
-    weights = scale_ref[...].astype(jnp.float32) / 4096.0
-    routes = routes_ref[...]
-
-    for expert in range(ep):
-        column = jnp.sum(jnp.where(routes == expert, weights, 0.0), axis=1, keepdims=True)
-        row = jnp.sum(jnp.where(lane == sub, column, 0.0), axis=0, keepdims=True)
-        WS[expert] = jnp.broadcast_to(row, (8, LANES))
-
     barrier = pltpu.get_barrier_semaphore()
 
     def greet(d, carry):
@@ -98,6 +82,22 @@
         return carry
 
     lax.fori_loop(1, n, greet, 0)
+
+    for copy in tile_copies(0, 0):
+        copy.start()
+
+    for h in range(2):
+        X[h, 0, rows(c, z), cols(x)] = tok_ref[h * hr:(h + 1) * hr, :]
+        X[h, 1, rows(c, z), cols(x)] = cot_ref[h * hr:(h + 1) * hr, :]
+    full = 2 * hr
+    weights = scale_ref[...].astype(jnp.float32) / 4096.0
+    routes = routes_ref[...]
+
+    WS[...] = jnp.zeros_like(WS)
+    for expert in range(ep):
+        row = jnp.sum(jnp.where(routes == expert, weights, 0.0), axis=0, keepdims=True)
+        WS[expert, :, 0:full] = jnp.broadcast_to(row, (8, full))
+
     rp[...] = jnp.zeros_like(rp)
     pl.semaphore_wait(barrier, n - 1)
 
@@ -212,8 +212,9 @@
     lax.fori_loop(1, ep, lambda d, carry: (bcopy(d).start(), carry)[1], 0)
     for s in range(1, nz):
         step(0, s)
+        if s == nz - 1:
+            own(1)
         xwait(0, s - 1)
-    own(1)
     xwait(0, nz - 1)
     lax.fori_loop(1, ep, lambda d, carry: (barrival(d).wait_recv(), carry)[1], 0)
     WR[e] = WS[e]
@@ -296,13 +297,10 @@
     def plan(i, fn):
         events.setdefault(i, []).append(fn)
 
-    for s in range(1, nz + 1):
-        def event(s=s):
-            if s < nz:
-                step(1, s)
-            xwait(1, s - 1)
-
-        plan(min(s, nt - 1), event)
+    for s in range(1, nz):
+        plan(min(s - 1, nt - 1), functools.partial(step, 1, s))
+    for s in range(nz):
+        plan(min(s + 1, nt - 1), functools.partial(xwait, 1, s))
     plan(nt, lambda: cwait(1))
 
     def first_chunks():
@@ -418,8 +416,7 @@
         row = jnp.zeros((1, LANES), jnp.float32)
         for xx in range(nx):
             row = row + RR[expert * nx + xx][0:1, :]
-        column = jnp.sum(jnp.where(lane == sub, row, 0.0), axis=1, keepdims=True)
-        grad = grad + jnp.where(routes == expert, column, 0.0)
+        grad = grad + jnp.where(routes == expert, row[:, 0:full], 0.0)
     rg_ref[...] = grad * (1.0 / math.sqrt(FF))
 
     for h in range(2):
@@ -450,17 +447,17 @@
     else:
         widths = [hidden]
     slots = min(2, len(widths))
-    cw = TILE if dx % TILE == 0 else dx
+    cw = CHUNK if dx % CHUNK == 0 else dx
     kc = dx // cw
     steps = kc * nx
     bf16, f32 = jnp.bfloat16, jnp.float32
     dma = pltpu.SemaphoreType.DMA
     vmem = pl.BlockSpec(memory_space=pltpu.VMEM)
-    return pl.pallas_call(
+    token_grad, route_grad = pl.pallas_call(
         functools.partial(kernel, nz, nx, widths),
         out_shape=(
             jax.ShapeDtypeStruct((block, dx), bf16),
-            jax.ShapeDtypeStruct(routes.shape, f32),
+            jax.ShapeDtypeStruct(routes.shape[::-1], f32),
         ),
         in_specs=[vmem] * 4 + [pl.BlockSpec(memory_space=pl.ANY)] * 3,
         out_specs=(vmem, vmem),
@@ -512,7 +509,8 @@
         cost_estimate=pl.CostEstimate(
             flops=20 * half * depth * hidden, bytes_accessed=12 * depth * hidden, transcendentals=0
         ),
-    )(tokens, cotangent, routes, route_scale, gate_weight, up_weight, down_weight)
+    )(tokens, cotangent, routes.T, route_scale.T, gate_weight, up_weight, down_weight)
+    return token_grad, route_grad.T
 
 
 def solution(mesh):

time: 119 us -> 113 us (0.950)
  Pallas kernels: 113 us -> 109 us
  local copies, waits for them, and re-layouts: 5.79 us -> 2.85 us
    pallas_call x1, Pallas kernels: 113 us -> 109 us  [shards(): pl.pallas_call(functools.partial(kernel, nz, nx, widths), out_shape=(jax....]
    unnamed x3 -> x2, local copies, waits for them, and re-layouts: 4.38 us -> 2.85 us
    pallas_call x1 -> x0, local copies, waits for them, and re-layouts: 1.41 us -> none  [shards(): pl.pallas_call(functools.partial(kernel, nz, nx, widths), out_shape=(jax....]
where the time goes in v3:
time: 113 us; the launch traced here: 112 us
  Pallas kernels  109 us (96%)
  local copies, waits for them, and re-layouts  2.85 us (3%)
    pallas_call x1, Pallas kernels, shards(): pl.pallas_call(functools.partial(kernel, nz, nx, widths), out_shape=(jax....  109 us
    unnamed x2, local copies, waits for them, and re-layouts  2.85 us

profile of v3, /device:TPU:0, one launch (start us, length us, event | category | flops | bytes accessed | tf_op | source)
XLA Modules:
  0.0 112.3 jit_solution(9786522903252119060)
XLA Ops:
  0.6 108.9 %shard_map.86 = (bf16[64,1536]{1,0:T(8,128)(2,1)}, f32[4,64]{1,0:T(4,128)}) custom-call(bf16[64,1536]{1,0:T(8,128)(2,1)} %tok_ref.1, bf16[64,1536]{1,0:T(8,128)(2,1)} %cot_ref.1, s32[4,64]{1,0:T(4,128)} %bitcast.4, s32[4,64]{1,0:T(4,128)} %bitcast.5, bf16[1,3072,2688]{2,1,0:T(8,128)(2,1)} %wg_hbm.1, bf16[1,3072,2688]{2,1,0:T(8,128)(2,1)} %wu_hbm.1, ...), custom_call_target="tpu_custom_call" | custom-call | flops 42278584320 | bytes 99090432 | tf_op jit(solution)/shard_map/pallas_call | solution.py:456
  109.5 1.6 %copy.11 = bf16[64,1536]{1,0:T(8,128)(2,1)} copy(bf16[64,1536]{1,0:T(8,128)(2,1)} %get-tuple-element.8) | data formatting | bytes 393216
  111.1 1.2 %copy.12 = f32[64,4]{0,1:T(4,128)} copy(f32[64,4]{0,1:T(4,128)} %bitcast.3) | data formatting | bytes 2048
